TPU v7x, 512 devices: a whole 4x4x16 slice. The times are simulated.
512 devices in a mesh: dp: 64 (over z, y_lo, core), tensor: 8 (over y_hi, x).
Axes of the slice: x: 4, y: 4 (y_hi: 2, y_lo: 2; y = y_hi * 2 + y_lo), z: 16, core: 2. Of those that a mesh axis runs over, the one named last changes fastest.
Arguments:
- gradient: bfloat16 [512, 262144], P(None, ('dp', 'tensor')), may hold values from -110 to 110
- owner_table: int32 [512], replicated, may hold values from 0 to 511, as said below
- prev_stats: bfloat16 [1024, 2, 512, 512], P(('dp', 'tensor')), may hold values from -16 to 8192, as said below
Outputs:
- update: bfloat16 [512, 262144], P(None, ('dp', 'tensor'))
Inputs may be any that keep to these rules, and one draw needn't show every extreme that they name: `owner_table`: a device index with dp major; a quarter of the devices own exactly 2 blocks each, a half own exactly half as many each, the remaining quarter own none. `prev_stats`: every matrix is symmetric and its diagonal entry exceeds the sum of the magnitudes of the other entries of its row; slots that no block takes are never read.
All inputs are finite; a program needn't handle non-finite values.
Results may differ from a plain program's by a relative error of at most 0.0014.
The roundings to bfloat16 on the way count: a program that leaves them out, or rounds other values in their place, can miss the bound.
Values may be sent and summed in bfloat16 or wider, within the bound.
A program may use at most 64 MiB of HBM per device.

v0:
```python
import jax
import jax.numpy as jnp
from jax import lax
from jax.sharding import PartitionSpec as P

BLK = 512
ITERS = 2


DECAY = 0.9
GRAFT_EPS = 1e-06


def batched_product(first, second):
    return jnp.einsum("...ij,...jk->...ik", first, second, preferred_element_type=jnp.float32)


def owner_rank(owner_table):
    block_count = owner_table.shape[0]
    positions = jnp.arange(block_count, dtype=jnp.int32)
    same_owner = owner_table[:, None] == owner_table[None, :]
    earlier = positions[None, :] < positions[:, None]
    return jnp.sum(jnp.where(same_owner & earlier, 1, 0), axis=1).astype(jnp.int32)


def inverse_roots(statistic):
    identity = jnp.eye(statistic.shape[-1], dtype=jnp.float32)
    norm_scale = jnp.sqrt(jnp.sum(statistic * statistic, axis=(-2, -1), keepdims=True))
    matrix = statistic / norm_scale
    root_est = statistic
    for sweep in range(ITERS):
        factor = (5.0 * identity - matrix) * 0.25
        if sweep == 0:
            root_est = norm_scale ** (-0.25) * factor
        else:
            root_est = batched_product(root_est.astype(jnp.bfloat16), factor.astype(jnp.bfloat16))
        if sweep + 1 < ITERS:
            factor_low = factor.astype(jnp.bfloat16)
            square_low = batched_product(factor_low, factor_low).astype(jnp.bfloat16)
            fourth = batched_product(square_low, square_low)
            matrix = batched_product(fourth.astype(jnp.bfloat16), matrix.astype(jnp.bfloat16))
    return root_est


def precondition(block_matrix, saved):
    left_gram = jnp.einsum(
        "cij,ckj->cik", block_matrix, block_matrix, preferred_element_type=jnp.float32
    )
    right_gram = jnp.einsum(
        "cji,cjk->cik", block_matrix, block_matrix, preferred_element_type=jnp.float32
    )
    statistic = DECAY * saved.astype(jnp.float32) + jnp.stack([left_gram, right_gram], axis=1)
    roots = inverse_roots(statistic).astype(jnp.bfloat16)
    middle = batched_product(block_matrix, roots[:, 1]).astype(jnp.bfloat16)
    return batched_product(roots[:, 0], middle).astype(jnp.bfloat16)


def on_device(gradient, owner_table, prev_stats):
    dp_size = lax.axis_size("dp")
    tensor_size = lax.axis_size("tensor")
    devices = dp_size * tensor_size
    capacity = prev_stats.shape[0]
    block_count, entries = gradient.shape
    slot_rank = owner_rank(owner_table)
    positions = jnp.arange(block_count, dtype=jnp.int32)
    inverse = (
        jnp.zeros((capacity * devices,), jnp.int32)
        .at[slot_rank * devices + owner_table]
        .set(positions)
    )
    outgoing = jnp.take(gradient, inverse, axis=0).reshape(capacity, dp_size, tensor_size, entries)
    received = lax.all_to_all(
        lax.all_to_all(outgoing, "dp", split_axis=1, concat_axis=1, tiled=True),
        "tensor",
        split_axis=2,
        concat_axis=2,
        tiled=True,
    )
    updates = precondition(received.reshape(capacity, BLK, BLK), prev_stats)
    returned = lax.all_to_all(
        lax.all_to_all(
            updates.reshape(capacity, dp_size, tensor_size, entries),
            "dp",
            split_axis=1,
            concat_axis=1,
            tiled=True,
        ),
        "tensor",
        split_axis=2,
        concat_axis=2,
        tiled=True,
    )
    flat_back = returned.reshape(capacity * devices, entries)
    mine = jnp.take(flat_back, slot_rank * devices + owner_table, axis=0)
    half_count = block_count // 2
    grad_sq = jnp.sum(
        jnp.sum(jnp.square(gradient.astype(jnp.float32)), axis=1).reshape(2, half_count), axis=1
    )
    update_sq = jnp.sum(
        jnp.sum(jnp.square(mine.astype(jnp.float32)), axis=1).reshape(2, half_count), axis=1
    )
    grad_total, update_total = lax.psum((grad_sq, update_sq), ("dp", "tensor"))
    graft_ratio = jnp.sqrt(grad_total / (update_total + GRAFT_EPS))
    per_row = jnp.where(positions < half_count, graft_ratio[0], graft_ratio[1])
    return (mine.astype(jnp.float32) * per_row[:, None]).astype(jnp.bfloat16)


def solution(mesh):
    in_specs = (P(None, ("dp", "tensor")), P(), P(("dp", "tensor"), None, None, None))
    out_specs = P(None, ("dp", "tensor"))
    return jax.shard_map(
        on_device, mesh=mesh, in_specs=in_specs, out_specs=out_specs, check_vma=False
    )
```

profile of v0, /device:TPU:1, one launch (start us, length us, event | category | flops | bytes accessed | tf_op | source)
XLA Modules:
  0.0 321.1 jit_solution(15278092952800045147)
XLA Ops:
  0.0 1.0 select_reduce_fusion
  1.7 2.4 scatter_custom_fusion
  4.3 5.1 %gather_fusion = bf16[1024,512]{1,0:T(8,128)(2,1)S(1)} fusion(bf16[512,512]{1,0:T(8,128)(2,1)} %param.3, s32[1024]{0:T(1024)S(1)} %fusion.34), kind=kCustom, calls=%fused_computation | custom fusion | bytes 2101248 | tf_op jit(solution)/shard_map/jit(_take)/gather | solution.py:71
  9.7 71.9 %all_to_all.20 = bf16[2,64,8,512]{3,2,0,1:T(8,128)(2,1)S(1)} all-to-all(bf16[2,64,8,512]{3,2,0,1:T(8,128)(2,1)S(1)} %copy_select_fusion), channel_id=1, replica_groups=mesh['dp'=64,'tensor'=8] {'dp'}, dimensions={1} | all-to-all | bytes 2097152 | tf_op jit(solution)/shard_map/all_to_all | solution.py:73
  81.6 1.6 copy.29
  83.1 6.4 %all-to-all-start.1 = ((bf16[2,64,8,512]{3,1,0,2:T(8,128)(2,1)}), bf16[2,64,8,512]{3,1,0,2:T(8,128)(2,1)S(1)}, u32[]{:S(2)}, u32[]{:S(2)}) async-start(bf16[2,64,8,512]{3,1,0,2:T(8,128)(2,1)} %copy.29), calls=%async_computation.1 | async-start | bytes 2097152 | tf_op jit(solution)/shard_map/all_to_all | solution.py:72
  89.5 1.2 fusion.25
  90.7 16.0 %all-to-all-done.1 = bf16[2,64,8,512]{3,1,0,2:T(8,128)(2,1)S(1)} async-done(((bf16[2,64,8,512]{3,1,0,2:T(8,128)(2,1)}), bf16[2,64,8,512]{3,1,0,2:T(8,128)(2,1)S(1)}, u32[]{:S(2)}, u32[]{:S(2)}) %all-to-all-start.1) | async-done | bytes 1048608 | tf_op jit(solution)/shard_map/all_to_all | solution.py:72
  106.7 1.5 convolution_bitcast_fusion
  108.2 1.3 convolution_bitcast_fusion.1
  109.8 0.9 multiply_reduce_fusion
  111.7 2.6 multiply_convert_fusion.2
  114.4 8.6 %fusion.9 = bf16[2,2,512,512]{3,2,1,0:T(8,128)(2,1)} fusion(bf16[2,2,512,512]{3,2,0,1:T(8,128)(2,1)} %get-tuple-element.10), kind=kOutput, calls=%fused_computation.18 | convolution fusion | flops 2149580800 | bytes 4194304 | tf_op jit(solution)/shard_map/...ij,...jk->...ik/dot_general | solution.py:15
  123.0 4.7 %multiply_convert_fusion = bf16[2,2,512,512]{3,2,0,1:T(8,128)(2,1)S(1)} fusion(bf16[2,2,512,512]{3,2,1,0:T(8,128)(2,1)} %fusion.9, f32[512,512]{1,0:T(8,128)} %fusion.25, f32[2,2]{0,1:T(2,128)S(1)} %get-tuple-element.12, f32[2,1,512,512]{3,2,0,1:T(8,128)S(1)} %convolution_bitcast_fusion, f32[2,1,512,512]{3,2,0,1:T(8,128)} %copy-done.1, ...), kind=kOutput, calls=%fused_computation.4 | convolution fusion | flops 1083179008 | bytes 11534352 | tf_op jit(solution)/shard_map/...ij,...jk->...ik/dot_general | solution.py:15
  127.7 2.6 fusion.12
  130.3 2.9 fusion.17
  133.4 59.8 %all_to_all.21 = bf16[2,64,8,512]{3,2,0,1:T(8,128)(2,1)S(1)} all-to-all(bf16[2,64,8,512]{3,2,0,1:T(8,128)(2,1)S(1)} %copy.37), channel_id=1, replica_groups=mesh['dp'=64,'tensor'=8] {'dp'}, dimensions={1} | all-to-all | bytes 2097152 | tf_op jit(solution)/shard_map/all_to_all | solution.py:81
  193.2 1.6 copy.38
  194.7 3.8 %all-to-all-start.3 = ((bf16[2,64,8,512]{3,1,0,2:T(8,128)(2,1)}), bf16[2,64,8,512]{3,1,0,2:T(8,128)(2,1)S(1)}, u32[]{:S(2)}, u32[]{:S(2)}) async-start(bf16[2,64,8,512]{3,1,0,2:T(8,128)(2,1)} %copy.38), calls=%async_computation.3 | async-start | bytes 2097152 | tf_op jit(solution)/shard_map/all_to_all | solution.py:80
  198.8 16.7 %all-to-all-done.3 = bf16[2,64,8,512]{3,1,0,2:T(8,128)(2,1)S(1)} async-done(((bf16[2,64,8,512]{3,1,0,2:T(8,128)(2,1)}), bf16[2,64,8,512]{3,1,0,2:T(8,128)(2,1)S(1)}, u32[]{:S(2)}, u32[]{:S(2)}) %all-to-all-start.3) | async-done | bytes 1048608 | tf_op jit(solution)/shard_map/all_to_all | solution.py:80
  216.1 2.0 gather_fusion.1
  218.5 99.6 %all-reduce = (f32[2]{0:T(128)S(1)}, f32[2]{0:T(128)S(1)}) all-reduce(f32[2]{0:T(128)S(1)} %reduce_sum.57, f32[2]{0:T(128)S(1)} %reduce_sum.59), channel_id=1, replica_groups=mesh['dp'=64,'tensor'=8] {'dp','tensor'}, use_global_device_ids=true, to_apply=%region_5.6 | all-reduce | flops 4 | bytes 32 | tf_op jit(solution)/shard_map/psum | solution.py:102
  318.8 1.3 fusion.37
  320.1 1.0 fusion.19
  (29 shorter events, 4.6 us)
Async XLA Ops:
  83.1 23.5 %all-to-all-start.1 = ((bf16[2,64,8,512]{3,1,0,2:T(8,128)(2,1)}), bf16[2,64,8,512]{3,1,0,2:T(8,128)(2,1)S(1)}, u32[]{:S(2)}, u32[]{:S(2)}) async-start(bf16[2,64,8,512]{3,1,0,2:T(8,128)(2,1)} %copy.29), calls=%async_computation.1 | async-start | bytes 2097152 | tf_op jit(solution)/shard_map/all_to_all | solution.py:72
  108.2 1.6 copy-start.2
  109.8 1.3 copy-start.1
  109.8 2.0 copy-start.3
  123.0 4.7 %copy-start.4 = (bf16[2,2,512,512]{3,2,0,1:T(8,128)(2,1)S(1)}, bf16[2,2,512,512]{3,2,0,1:T(8,128)(2,1)}, u32[]{:S(2)}) copy-start(bf16[2,2,512,512]{3,2,0,1:T(8,128)(2,1)} %get-tuple-element.9) | copy-start | bytes 6291460
  193.1 5.4 %copy-start = (bf16[512,512]{1,0:T(8,128)(2,1)S(1)}, bf16[512,512]{1,0:T(8,128)(2,1)}, u32[]{:S(2)}) copy-start(bf16[512,512]{1,0:T(8,128)(2,1)} %param.3) | copy-start | bytes 1572868
  194.7 20.8 %all-to-all-start.3 = ((bf16[2,64,8,512]{3,1,0,2:T(8,128)(2,1)}), bf16[2,64,8,512]{3,1,0,2:T(8,128)(2,1)S(1)}, u32[]{:S(2)}, u32[]{:S(2)}) async-start(bf16[2,64,8,512]{3,1,0,2:T(8,128)(2,1)} %copy.38), calls=%async_computation.3 | async-start | bytes 2097152 | tf_op jit(solution)/shard_map/all_to_all | solution.py:80
where the time goes:
time: 322 us; the launch traced here: 321 us
  blocking collectives  231 us (72%)
  waiting for transfers between devices  32.7 us (10%)
  matrix products  21.6 us (7%)
  local copies, waits for them, and re-layouts  15.6 us (5%)
  starting transfers between devices  10.1 us (3%)
  other arithmetic  9.73 us (3%)
    psum x1, blocking collectives, on_device(): grad_total, update_total = lax.psum((grad_sq, update_sq), ('dp', 'tensor'))  99.6 us
    all_to_all x1, blocking collectives, on_device(): lax.all_to_all(outgoing, 'dp', split_axis=1, concat_axis=1, tiled=True)  71.9 us
    all_to_all x1, blocking collectives, on_device(): lax.all_to_all(updates.reshape(capacity, dp_size, tensor_size, entries),...  59.8 us
    dot_general x4, matrix products, batched_product(): jnp.einsum('...ij,...jk->...ik', first, second, preferred_element_type=jn...  18.8 us
    all_to_all x1, waiting for transfers between devices, on_device(): lax.all_to_all(lax.all_to_all(updates.reshape(capacity, dp_size, tensor_s...  16.7 us
    all_to_all x1, waiting for transfers between devices, on_device(): lax.all_to_all(lax.all_to_all(outgoing, 'dp', split_axis=1, concat_axis=1...  16 us
  transfers between devices with their start and end apart: 2, of which 2 were waited for; matrix products, arithmetic and copies ran while one was open for 0% of the time, Pallas kernels for 0%

commit v1 on v0

v1 whole, which is shorter than its diff:
```python
import jax
import jax.numpy as jnp
from jax import lax
from jax.experimental import pallas as pl
from jax.experimental.pallas import tpu as pltpu
from jax.sharding import PartitionSpec as P

BLK = 512
ITERS = 2
DECAY = 0.9
GRAFT_EPS = 1e-06

NZ = 16
NQ = 4
NT = 8
NP = NQ * NT
CAP1 = 16

MESH = pl.DeviceIdType.MESH
F32 = jnp.float32
BF16 = jnp.bfloat16


def batched_product(first, second):
    return jnp.einsum("...ij,...jk->...ik", first, second, preferred_element_type=F32)


def owner_rank(owner_table):
    block_count = owner_table.shape[0]
    positions = jnp.arange(block_count, dtype=jnp.int32)
    same_owner = owner_table[:, None] == owner_table[None, :]
    earlier = positions[None, :] < positions[:, None]
    return jnp.sum(jnp.where(same_owner & earlier, 1, 0), axis=1).astype(jnp.int32)


def inverse_roots(statistic):
    identity = jnp.eye(statistic.shape[-1], dtype=F32)
    norm_scale = jnp.sqrt(jnp.sum(statistic * statistic, axis=(-2, -1), keepdims=True))
    matrix = statistic / norm_scale
    root_est = statistic
    for sweep in range(ITERS):
        factor = (5.0 * identity - matrix) * 0.25
        if sweep == 0:
            root_est = norm_scale ** (-0.25) * factor
        else:
            root_est = batched_product(root_est.astype(BF16), factor.astype(BF16))
        if sweep + 1 < ITERS:
            factor_low = factor.astype(BF16)
            square_low = batched_product(factor_low, factor_low).astype(BF16)
            fourth = batched_product(square_low, square_low)
            matrix = batched_product(fourth.astype(BF16), matrix.astype(BF16))
    return root_est


def precondition(block_matrix, saved):
    left_gram = jnp.einsum("cij,ckj->cik", block_matrix, block_matrix, preferred_element_type=F32)
    right_gram = jnp.einsum("cji,cjk->cik", block_matrix, block_matrix, preferred_element_type=F32)
    statistic = DECAY * saved.astype(F32) + jnp.stack([left_gram, right_gram], axis=1)
    roots = inverse_roots(statistic).astype(BF16)
    middle = batched_product(block_matrix, roots[:, 1]).astype(BF16)
    return batched_product(roots[:, 0], middle).astype(BF16)


def general_program(gradient, owner_table, prev_stats):
    dp_size = lax.axis_size("dp")
    tensor_size = lax.axis_size("tensor")
    devices = dp_size * tensor_size
    capacity = prev_stats.shape[0]
    block_count, entries = gradient.shape
    slot_rank = owner_rank(owner_table)
    positions = jnp.arange(block_count, dtype=jnp.int32)
    inverse = (
        jnp.zeros((capacity * devices,), jnp.int32)
        .at[slot_rank * devices + owner_table]
        .set(positions)
    )
    outgoing = jnp.take(gradient, inverse, axis=0).reshape(capacity, dp_size, tensor_size, entries)

    def exchange(rows):
        rows = lax.all_to_all(rows, "dp", split_axis=1, concat_axis=1, tiled=True)
        return lax.all_to_all(rows, "tensor", split_axis=2, concat_axis=2, tiled=True)

    received = exchange(outgoing)
    updates = precondition(received.reshape(capacity, BLK, BLK), prev_stats)
    returned = exchange(updates.reshape(capacity, dp_size, tensor_size, entries))
    flat_back = returned.reshape(capacity * devices, entries)
    mine = jnp.take(flat_back, slot_rank * devices + owner_table, axis=0)
    half_count = block_count // 2
    grad_sq = jnp.sum(
        jnp.sum(jnp.square(gradient.astype(F32)), axis=1).reshape(2, half_count), axis=1
    )
    update_sq = jnp.sum(
        jnp.sum(jnp.square(mine.astype(F32)), axis=1).reshape(2, half_count), axis=1
    )
    grad_total, update_total = lax.psum((grad_sq, update_sq), ("dp", "tensor"))
    graft_ratio = jnp.sqrt(grad_total / (update_total + GRAFT_EPS))
    per_row = jnp.where(positions < half_count, graft_ratio[0], graft_ratio[1])
    return (mine.astype(F32) * per_row[:, None]).astype(BF16)


def iota(shape, dim):
    return lax.broadcasted_iota(jnp.int32, shape, dim)


def ones_where(mask):
    return jnp.where(mask, 1.0, 0.0)


def dot(a, b):
    return jnp.dot(a, b, preferred_element_type=F32)


def dot_t(a, b):
    return lax.dot_general(a, b, (((1,), (1,)), ((), ())), preferred_element_type=F32)


def kernel(
    grad_ref,
    owner_ref,
    stats_ref,
    out_ref,
    flag_ref,
    stats_v,
    stat_sem,
    za_send, za_recv, zb_send, zb_recv,
    pa_send, pa_recv, pb_send, pb_recv,
    ra_send, ra_recv, rb_send, rb_recv,
    ya_send, ya_recv, yb_send, yb_recv,
    norm_mine, norm_plane, plane_mine, plane_all,
    fold_ref, unfold_ref, ohm_ref, ohmt_ref, fin0_ref, fin1_ref,
    block_ref, root_ref,
    z_ssem, z_rsem, p_ssem, p_rsem,
):
    dp = lax.axis_index("dp")
    t = lax.axis_index("tensor")
    z = dp // NQ
    q = lax.rem(dp, NQ)
    p = q * NT + t
    me = z * NP + p

    stat_copy = pltpu.make_async_copy(stats_ref, stats_v, stat_sem)
    stat_copy.start()

    def z_peer(k):
        half = k // 2
        off = jnp.where(lax.rem(k, 2) == 0, 8 + half, 8 - half)
        return off, lax.rem(z + off, NZ)

    def p_peer(k):
        return lax.rem(p + k, NP)

    barrier = pltpu.get_barrier_semaphore()

    def greet_z(k, c):
        _, zt = z_peer(k)
        pl.semaphore_signal(barrier, inc=1, device_id=(zt * NQ + q, t), device_id_type=MESH)
        return c

    def greet_p(k, c):
        pt = p_peer(k)
        pl.semaphore_signal(
            barrier, inc=1, device_id=(z * NQ + pt // NT, lax.rem(pt, NT)), device_id_type=MESH
        )
        return c

    lax.fori_loop(1, NZ, greet_z, 0)
    lax.fori_loop(1, NP, greet_p, 0)

    def z_copy(phase, k, src, dst, whole):
        off, zt = z_peer(k)
        return pltpu.make_async_remote_copy(
            src_ref=src if whole else src.at[zt],
            dst_ref=dst.at[z],
            send_sem=z_ssem.at[phase, off],
            recv_sem=z_rsem.at[phase, off],
            device_id=(zt * NQ + q, t),
            device_id_type=MESH,
        )

    def p_copy(phase, k, src, dst, whole):
        pt = p_peer(k)
        return pltpu.make_async_remote_copy(
            src_ref=src if whole else src.at[pt],
            dst_ref=dst.at[p],
            send_sem=p_ssem.at[phase, k],
            recv_sem=p_rsem.at[phase, k],
            device_id=(z * NQ + pt // NT, lax.rem(pt, NT)),
            device_id_type=MESH,
        )

    def start(make, count, phase, src, dst, whole=False):
        def step(k, c):
            make(phase, k, src, dst, whole).start()
            return c

        lax.fori_loop(1, count, step, 0)
        if make is z_copy:
            dst[pl.ds(z, 1)] = src[...][None] if whole else src[pl.ds(z, 1)]
        else:
            dst[pl.ds(p, 1)] = src[...][None] if whole else src[pl.ds(p, 1)]

    def arrive(make, count, phase, src, dst, whole=False):
        def step(k, c):
            make(phase, k, src, dst, whole).wait_recv()
            return c

        lax.fori_loop(1, count, step, 0)

    def drain(make, count, phase, src, dst, whole=False):
        def step(k, c):
            make(phase, k, src, dst, whole).wait_send()
            return c

        lax.fori_loop(1, count, step, 0)

    n = BLK
    i0 = iota((n, n), 0)
    i1 = iota((n, n), 1)
    owner_row = owner_ref[...].astype(F32)
    owner_col = jnp.sum(jnp.where(i0 == i1, owner_row, 0.0), axis=1, keepdims=True)
    same = owner_col == owner_row
    rank_row = jnp.sum(ones_where(same & (i0 < i1)), axis=0, keepdims=True)
    rank_col = jnp.sum(ones_where(same & (i1 < i0)), axis=1, keepdims=True)
    plane_row = jnp.floor(owner_row * (1.0 / NP))
    plane_col = jnp.floor(owner_col * (1.0 / NP))
    second_row = jnp.where(rank_row > 0.5, plane_row, -1.0)
    second_col = jnp.where(rank_col > 0.5, plane_col, -2.0)
    second_col_b = jnp.where(rank_col > 0.5, plane_col, -1.0)
    second_row_b = jnp.where(rank_row > 0.5, plane_row, -2.0)
    pos_row = jnp.sum(ones_where((second_col == second_row) & (i0 < i1)), axis=0, keepdims=True)
    pos_col = jnp.sum(ones_where((second_col_b == second_row_b) & (i1 < i0)), axis=1, keepdims=True)

    first_row = jnp.where(rank_row < 0.5, owner_row, -1.0)
    first_col = jnp.where(rank_col < 0.5, owner_col, -1.0)
    late_row = jnp.where(
        (rank_row > 0.5) & (pos_row < CAP1 - 0.5), plane_row * CAP1 + pos_row, -1.0
    )
    late_col = jnp.where(
        (rank_col > 0.5) & (pos_col < CAP1 - 0.5), plane_col * CAP1 + pos_col, -1.0
    )
    f0 = i0.astype(F32)
    f1 = i1.astype(F32)

    pick1 = ones_where(late_row == f0[: NZ * CAP1]).astype(BF16)
    zb_send[...] = dot(pick1, grad_ref[...]).astype(BF16).reshape(NZ, CAP1, n)
    pick0 = ones_where(first_row == f0).astype(BF16)
    za_send[...] = dot(pick0, grad_ref[...]).astype(BF16).reshape(NZ, NP, n)

    pl.semaphore_wait(barrier, NZ - 1 + NP - 1)
    start(z_copy, NZ, 0, zb_send, zb_recv)
    start(z_copy, NZ, 1, za_send, za_recv)

    fin0_ref[...] = ones_where(first_col == f1).astype(BF16)
    fin1_ref[...] = ones_where(late_col == f1[:, : NZ * CAP1]).astype(BF16)
    overflow = jnp.max(jnp.where(rank_row > 0.5, pos_row, 0.0), axis=1, keepdims=True)
    flag_ref[...] = jnp.broadcast_to(overflow, flag_ref.shape)

    to_zp = (i0 & (NZ - 1)) * NP + lax.shift_right_logical(i0, 4)
    to_zp_t = (i1 & (NZ - 1)) * NP + lax.shift_right_logical(i1, 4)
    fold_ref[...] = ones_where(to_zp == i1).astype(BF16)
    unfold_ref[...] = ones_where(to_zp_t == i0).astype(BF16)

    z_base = (z * NP).astype(F32)
    dev_of = z_base + lax.shift_right_logical(i0, 4).astype(F32)
    dev_of_t = z_base + lax.shift_right_logical(i1, 4).astype(F32)
    held_row = jnp.where(rank_row > 0.5, owner_row, -1.0)
    held_col = jnp.where(rank_col > 0.5, owner_col, -1.0)
    at_col = jnp.sum(jnp.where(held_row == dev_of, pos_row + 1.0, 0.0), axis=1, keepdims=True)
    at_row = jnp.sum(jnp.where(held_col == dev_of_t, pos_col + 1.0, 0.0), axis=0, keepdims=True)
    m = NZ * CAP1
    a0, a1 = iota((n, m), 0), iota((n, m), 1)
    ohm_ref[...] = ones_where(
        (lax.shift_right_logical(a1, 4) == (a0 & (NZ - 1)))
        & ((a1 & (CAP1 - 1)).astype(F32) == at_col - 1.0)
    ).astype(BF16)
    c0, c1 = iota((m, n), 0), iota((m, n), 1)
    ohmt_ref[...] = ones_where(
        (lax.shift_right_logical(c0, 4) == (c1 & (NZ - 1)))
        & ((c0 & (CAP1 - 1)).astype(F32) == at_row - 1.0)
    ).astype(BF16)

    me_f = me.astype(F32)
    lane = iota((1, n), 1)

    def slot_facts(slot):
        here = (owner_row == me_f) & (jnp.abs(rank_row - slot) < 0.5)
        used = jnp.sum(ones_where(here), axis=1, keepdims=True)
        layer1 = jnp.sum(ones_where(here & (lane >= n // 2)), axis=1, keepdims=True)
        return used, layer1

    identity5 = jnp.where(i0 == i1, 1.25, 0.0)

    def inverse_root(stat):
        total = jnp.sum(jnp.sum(stat * stat, axis=1, keepdims=True), axis=0, keepdims=True)
        norm_scale = jnp.sqrt(total)
        matrix = stat * (1.0 / norm_scale)
        factor = identity5 - 0.25 * matrix
        low = factor.astype(BF16)
        root = (lax.rsqrt(jnp.sqrt(norm_scale)) * factor).astype(BF16)
        square = dot(low, low).astype(BF16)
        fourth = dot(square, square).astype(BF16)
        matrix = dot(fourth, matrix.astype(BF16))
        factor = (identity5 - 0.25 * matrix).astype(BF16)
        return dot(root, factor).astype(BF16)

    def owner_work(slot, incoming, outgoing):
        block = dot(unfold_ref[...], incoming[...].reshape(n, n)).astype(BF16)
        block_ref[...] = block
        eye = ones_where(i0 == i1).astype(BF16)
        block_t = dot_t(eye, block).astype(BF16)
        right = inverse_root(DECAY * stats_v[slot, 1].astype(F32) + dot_t(block_t, block_t))
        middle = dot(block_ref[...], right).astype(BF16)
        left = inverse_root(
            DECAY * stats_v[slot, 0].astype(F32) + dot_t(block_ref[...], block_ref[...])
        )
        raw = dot(left, middle)
        used, layer1 = slot_facts(slot)
        raw = jnp.where(used > 0.5, raw, 0.0).astype(BF16)
        root_ref[...] = raw
        outgoing[...] = dot(fold_ref[...], root_ref[...]).astype(BF16).reshape(NP, NZ, n)
        raw_f = root_ref[...].astype(F32)
        update_sq = jnp.sum(jnp.sum(raw_f * raw_f, axis=1, keepdims=True), axis=0, keepdims=True)
        block_f = block_ref[...].astype(F32)
        grad_sq = jnp.sum(jnp.sum(block_f * block_f, axis=1, keepdims=True), axis=0, keepdims=True)
        g1 = jnp.where(layer1 > 0.5, grad_sq, 0.0)
        u1 = jnp.where(layer1 > 0.5, update_sq, 0.0)
        return grad_sq - g1, g1, update_sq - u1, u1

    arrive(z_copy, NZ, 0, zb_send, zb_recv)
    pb_send[...] = dot(ohm_ref[...], zb_recv[...].reshape(m, n)).astype(BF16).reshape(NP, NZ, n)
    start(p_copy, NP, 0, pb_send, pb_recv)
    stat_copy.wait()
    arrive(p_copy, NP, 0, pb_send, pb_recv)
    sums1 = owner_work(1, pb_recv, rb_send)
    start(p_copy, NP, 2, rb_send, rb_recv)

    arrive(z_copy, NZ, 1, za_send, za_recv)
    pa_send[...] = dot(fold_ref[...], za_recv[...].reshape(n, n)).astype(BF16).reshape(NP, NZ, n)
    start(p_copy, NP, 1, pa_send, pa_recv)

    arrive(p_copy, NP, 2, rb_send, rb_recv)
    yb_send[...] = dot(ohmt_ref[...], rb_recv[...].reshape(n, n)).astype(BF16).reshape(NZ, CAP1, n)
    start(z_copy, NZ, 2, yb_send, yb_recv)

    arrive(p_copy, NP, 1, pa_send, pa_recv)
    sums0 = owner_work(0, pa_recv, ra_send)
    start(p_copy, NP, 3, ra_send, ra_recv)
    s0 = iota((8, 128), 0)
    tile = jnp.zeros((8, 128), F32)
    for r in range(4):
        tile = jnp.where(s0 == r, sums0[r] + sums1[r], tile)
    norm_mine[...] = tile
    start(p_copy, NP, 4, norm_mine, norm_plane, whole=True)

    arrive(p_copy, NP, 3, ra_send, ra_recv)
    ya_send[...] = dot(unfold_ref[...], ra_recv[...].reshape(n, n)).astype(BF16).reshape(NZ, NP, n)
    start(z_copy, NZ, 3, ya_send, ya_recv)

    arrive(p_copy, NP, 4, norm_mine, norm_plane, whole=True)
    plane_mine[...] = jnp.sum(norm_plane[...], axis=0)
    start(z_copy, NZ, 4, plane_mine, plane_all, whole=True)

    arrive(z_copy, NZ, 2, yb_send, yb_recv)
    late = dot(fin1_ref[...], yb_recv[...].reshape(m, n))
    arrive(z_copy, NZ, 4, plane_mine, plane_all, whole=True)
    totals = jnp.sum(plane_all[...], axis=0)
    ratio0 = jnp.sqrt(totals[0:1, 0:1] / (totals[2:3, 0:1] + GRAFT_EPS))
    ratio1 = jnp.sqrt(totals[1:2, 0:1] / (totals[3:4, 0:1] + GRAFT_EPS))
    ratio = jnp.where(iota((n, 1), 0) < n // 2, ratio0, ratio1)
    arrive(z_copy, NZ, 3, ya_send, ya_recv)
    rows = dot(fin0_ref[...], ya_recv[...].reshape(n, n)) + late
    out_ref[...] = (rows * ratio).astype(BF16)

    drain(z_copy, NZ, 0, zb_send, zb_recv)
    drain(z_copy, NZ, 1, za_send, za_recv)
    drain(z_copy, NZ, 2, yb_send, yb_recv)
    drain(z_copy, NZ, 3, ya_send, ya_recv)
    drain(z_copy, NZ, 4, plane_mine, plane_all, whole=True)
    drain(p_copy, NP, 0, pb_send, pb_recv)
    drain(p_copy, NP, 1, pa_send, pa_recv)
    drain(p_copy, NP, 2, rb_send, rb_recv)
    drain(p_copy, NP, 3, ra_send, ra_recv)
    drain(p_copy, NP, 4, norm_mine, norm_plane, whole=True)


def fast_program(gradient, owner_table, prev_stats):
    n = BLK
    za, zb = pltpu.VMEM((NZ, NP, n), BF16), pltpu.VMEM((NZ, CAP1, n), BF16)
    pp = pltpu.VMEM((NP, NZ, n), BF16)
    square = pltpu.VMEM((n, n), BF16)
    vmem = pl.BlockSpec(memory_space=pltpu.VMEM)
    return pl.pallas_call(
        kernel,
        out_shape=(
            jax.ShapeDtypeStruct((n, n), BF16),
            jax.ShapeDtypeStruct((8, 128), F32),
        ),
        in_specs=[vmem, vmem, pl.BlockSpec(memory_space=pl.ANY)],
        out_specs=(vmem, vmem),
        scratch_shapes=[
            pltpu.VMEM((2, 2, n, n), BF16),
            pltpu.SemaphoreType.DMA,
            za, za, zb, zb,
            pp, pp, pp, pp,
            pp, pp, pp, pp,
            za, za, zb, zb,
            pltpu.VMEM((8, 128), F32),
            pltpu.VMEM((NP, 8, 128), F32),
            pltpu.VMEM((8, 128), F32),
            pltpu.VMEM((NZ, 8, 128), F32),
            square, square,
            pltpu.VMEM((n, NZ * CAP1), BF16),
            pltpu.VMEM((NZ * CAP1, n), BF16),
            square,
            pltpu.VMEM((n, NZ * CAP1), BF16),
            square, square,
            pltpu.SemaphoreType.DMA((5, NZ)),
            pltpu.SemaphoreType.DMA((5, NZ)),
            pltpu.SemaphoreType.DMA((5, NP)),
            pltpu.SemaphoreType.DMA((5, NP)),
        ],
        compiler_params=pltpu.CompilerParams(
            collective_id=0, has_side_effects=True, vmem_limit_bytes=56 << 20
        ),
    )(gradient, owner_table.reshape(1, -1), prev_stats)


def on_device(gradient, owner_table, prev_stats):
    update, overflow = fast_program(gradient, owner_table, prev_stats)
    return lax.cond(
        overflow[0, 0] > CAP1 - 0.5,
        lambda g, o, s, u: general_program(g, o, s),
        lambda g, o, s, u: u,
        gradient,
        owner_table,
        prev_stats,
        update,
    )


def solution(mesh):
    in_specs = (P(None, ("dp", "tensor")), P(), P(("dp", "tensor"), None, None, None))
    out_specs = P(None, ("dp", "tensor"))
    return jax.shard_map(
        on_device, mesh=mesh, in_specs=in_specs, out_specs=out_specs, check_vma=False
    )
```

time: 322 us -> 119 us (0.37)
  blocking collectives: 231 us -> 0 us
  Pallas kernels: 0 us -> 115 us
  waiting for transfers between devices: 32.7 us -> 0 us
  matrix products: 21.6 us -> 0 us
  local copies, waits for them, and re-layouts: 15.6 us -> 2 us
  starting transfers between devices: 10.1 us -> 0 us
  other arithmetic: 9.73 us -> 0 us
    all_to_all x2 -> x0, blocking collectives: 132 us -> none  [the longest x1 71.9 us: on_device(): lax.all_to_all(outgoing, 'dp', split_axis=1, concat_axis=1, tiled=True)]
    pallas_call x0 -> x1, Pallas kernels: none -> 115 us  [fast_program(): pl.pallas_call(kernel, out_shape=(jax.ShapeDtypeStruct((n, n), BF16), jax...]
    psum x1 -> x0, blocking collectives: 99.6 us -> none  [on_device(): grad_total, update_total = lax.psum((grad_sq, update_sq), ('dp', 'tensor'))]
    all_to_all x2 -> x0, waiting for transfers between devices: 32.7 us -> none  [the longest x1 16.7 us: on_device(): lax.all_to_all(lax.all_to_all(updates.reshape(capacity, dp_size, tensor_s...]
    dot_general x6 -> x0, matrix products: 21.6 us -> none  [the longest x4 18.8 us: batched_product(): jnp.einsum('...ij,...jk->...ik', first, second, preferred_element_type=jn...]
    all_to_all x2 -> x0, starting transfers between devices: 10.1 us -> none  [the longest x1 6.36 us: on_device(): lax.all_to_all(lax.all_to_all(outgoing, 'dp', split_axis=1, concat_axis=1...]
    gather x2 -> x0, local copies, waits for them, and re-layouts: 7.07 us -> none  [the longest x1 5.1 us: on_device(): jnp.take(gradient, inverse, axis=0)]
    all_to_all x3 -> x0, local copies, waits for them, and re-layouts: 3.72 us -> none  [the longest x1 1.57 us: on_device(): lax.all_to_all(outgoing, 'dp', split_axis=1, concat_axis=1, tiled=True)]
  transfers between devices with their start and end apart: 2 -> 0, of which waited for: 2 -> 0; matrix products, arithmetic and copies ran while one was open for 0% -> 0% of each run, Pallas kernels for 0% -> 0%
where the time goes in v1:
time: 119 us; the launch traced here: 118 us
  Pallas kernels  115 us (97%)
  local copies, waits for them, and re-layouts  2 us (2%)
    pallas_call x1, Pallas kernels, fast_program(): pl.pallas_call(kernel, out_shape=(jax.ShapeDtypeStruct((n, n), BF16), jax...  115 us

profile of v1, /device:TPU:1, one launch (start us, length us, event | category | flops | bytes accessed | tf_op | source)
XLA Modules:
  0.0 117.9 jit_solution(3354337517023874981)
XLA Ops:
  0.0 0.0 copy-start.6
  0.0 0.0 copy-start
  0.0 0.0 copy-start.1
  0.0 115.0 %shard_map.39 = (bf16[512,512]{1,0:T(8,128)(2,1)S(1)}, f32[8,128]{1,0:T(8,128)}) custom-call(bf16[512,512]{1,0:T(8,128)(2,1)} %grad_ref.1, s32[1,512]{1,0:T(1,128)} %bitcast.30, bf16[2,2,512,512]{3,2,1,0:T(8,128)(2,1)} %stats_ref.1), custom_call_target="tpu_custom_call" | custom-call | tf_op jit(solution)/shard_map/pallas_call | solution.py:392
  115.0 1.2 %slice.15 = f32[1,1]{1,0:T(1,128)} slice(f32[8,128]{1,0:T(8,128)} %get-tuple-element.20), slice={[0:1], [0:1]} | slice | bytes 8 | tf_op jit(solution)/shard_map/slice | solution.py:431
  116.8 0.0 copy-done.6
  116.9 0.0 copy-done
  116.9 0.0 copy-done.1
  116.9 0.3 conditional.1
  117.1 0.8 copy.88
Async XLA Ops:
  0.0 116.8 %copy-start.6 = (s32[512]{0:T(512)S(1)}, s32[512]{0:T(512)}, u32[]{:S(2)}) copy-start(s32[512]{0:T(512)} %param.6) | copy-start | bytes 6148
  0.0 116.9 %copy-start = (bf16[512,512]{1,0:T(8,128)(2,1)S(1)}, bf16[512,512]{1,0:T(8,128)(2,1)}, u32[]{:S(2)}) copy-start(bf16[512,512]{1,0:T(8,128)(2,1)} %grad_ref.1) | copy-start | bytes 1572868
  0.0 116.9 %copy-start.1 = (bf16[2,2,512,512]{3,2,1,0:T(8,128)(2,1)S(1)}, bf16[2,2,512,512]{3,2,1,0:T(8,128)(2,1)}, u32[]{:S(2)}) copy-start(bf16[2,2,512,512]{3,2,1,0:T(8,128)(2,1)} %stats_ref.1) | copy-start | bytes 6291460

commit v2 on v1

v2 whole, which is shorter than its diff:
```python
import jax
import jax.numpy as jnp
from jax import lax
from jax.experimental import pallas as pl
from jax.experimental.pallas import tpu as pltpu
from jax.sharding import PartitionSpec as P

BLK = 512
ITERS = 2
DECAY = 0.9
GRAFT_EPS = 1e-06

NZ = 16
NQ = 4
NT = 8
NP = NQ * NT
HALF = 16
CAP1 = 16

MESH = pl.DeviceIdType.MESH
F32 = jnp.float32
BF16 = jnp.bfloat16


def batched_product(first, second):
    return jnp.einsum("...ij,...jk->...ik", first, second, preferred_element_type=F32)


def owner_rank(owner_table):
    block_count = owner_table.shape[0]
    positions = jnp.arange(block_count, dtype=jnp.int32)
    same_owner = owner_table[:, None] == owner_table[None, :]
    earlier = positions[None, :] < positions[:, None]
    return jnp.sum(jnp.where(same_owner & earlier, 1, 0), axis=1).astype(jnp.int32)


def inverse_roots(statistic):
    identity = jnp.eye(statistic.shape[-1], dtype=F32)
    norm_scale = jnp.sqrt(jnp.sum(statistic * statistic, axis=(-2, -1), keepdims=True))
    matrix = statistic / norm_scale
    root_est = statistic
    for sweep in range(ITERS):
        factor = (5.0 * identity - matrix) * 0.25
        if sweep == 0:
            root_est = norm_scale ** (-0.25) * factor
        else:
            root_est = batched_product(root_est.astype(BF16), factor.astype(BF16))
        if sweep + 1 < ITERS:
            factor_low = factor.astype(BF16)
            square_low = batched_product(factor_low, factor_low).astype(BF16)
            fourth = batched_product(square_low, square_low)
            matrix = batched_product(fourth.astype(BF16), matrix.astype(BF16))
    return root_est


def precondition(block_matrix, saved):
    left_gram = jnp.einsum("cij,ckj->cik", block_matrix, block_matrix, preferred_element_type=F32)
    right_gram = jnp.einsum("cji,cjk->cik", block_matrix, block_matrix, preferred_element_type=F32)
    statistic = DECAY * saved.astype(F32) + jnp.stack([left_gram, right_gram], axis=1)
    roots = inverse_roots(statistic).astype(BF16)
    middle = batched_product(block_matrix, roots[:, 1]).astype(BF16)
    return batched_product(roots[:, 0], middle).astype(BF16)


def general_program(gradient, owner_table, prev_stats):
    dp_size = lax.axis_size("dp")
    tensor_size = lax.axis_size("tensor")
    devices = dp_size * tensor_size
    capacity = prev_stats.shape[0]
    block_count, entries = gradient.shape
    slot_rank = owner_rank(owner_table)
    positions = jnp.arange(block_count, dtype=jnp.int32)
    inverse = (
        jnp.zeros((capacity * devices,), jnp.int32)
        .at[slot_rank * devices + owner_table]
        .set(positions)
    )
    outgoing = jnp.take(gradient, inverse, axis=0).reshape(capacity, dp_size, tensor_size, entries)

    def exchange(rows):
        rows = lax.all_to_all(rows, "dp", split_axis=1, concat_axis=1, tiled=True)
        return lax.all_to_all(rows, "tensor", split_axis=2, concat_axis=2, tiled=True)

    received = exchange(outgoing)
    updates = precondition(received.reshape(capacity, BLK, BLK), prev_stats)
    returned = exchange(updates.reshape(capacity, dp_size, tensor_size, entries))
    flat_back = returned.reshape(capacity * devices, entries)
    mine = jnp.take(flat_back, slot_rank * devices + owner_table, axis=0)
    half_count = block_count // 2
    grad_sq = jnp.sum(
        jnp.sum(jnp.square(gradient.astype(F32)), axis=1).reshape(2, half_count), axis=1
    )
    update_sq = jnp.sum(
        jnp.sum(jnp.square(mine.astype(F32)), axis=1).reshape(2, half_count), axis=1
    )
    grad_total, update_total = lax.psum((grad_sq, update_sq), ("dp", "tensor"))
    graft_ratio = jnp.sqrt(grad_total / (update_total + GRAFT_EPS))
    per_row = jnp.where(positions < half_count, graft_ratio[0], graft_ratio[1])
    return (mine.astype(F32) * per_row[:, None]).astype(BF16)


def iota(shape, dim):
    return lax.broadcasted_iota(jnp.int32, shape, dim)


def ones_where(mask):
    return jnp.where(mask, 1.0, 0.0)


def dot(a, b):
    return jnp.dot(a, b, preferred_element_type=F32)


def dot_t(a, b):
    return lax.dot_general(a, b, (((1,), (1,)), ((), ())), preferred_element_type=F32)


def kernel(
    grad_hbm,
    owner_ref,
    stats_hbm,
    out_ref,
    flag_ref,
    grad_v, stats_v,
    z_out, z_in,
    pb_out, pb_in, pa_out, pa_in,
    rb_out, rb_in, ra_out, ra_in,
    y_out, y_in,
    norm_mine, norm_plane, plane_mine, plane_all,
    fold_ref, unfold_ref, fold_half, unfold_half, place_ref, place_t_ref, final_ref,
    block_ref, raw_ref, rows_ref,
    load_sem, z_ssem, z_rsem, p_ssem, p_rsem,
):
    dp = lax.axis_index("dp")
    t = lax.axis_index("tensor")
    z = dp // NQ
    q = lax.rem(dp, NQ)
    core = lax.rem(q, 2)
    p = q * NT + t
    j = (q // 2) * NT + t
    me = z * NP + p
    n = BLK
    m = NZ * HALF

    grad_copy = pltpu.make_async_copy(grad_hbm, grad_v, load_sem.at[0])
    stat_copy = pltpu.make_async_copy(stats_hbm, stats_v, load_sem.at[1])
    grad_copy.start()

    def z_peer(k):
        half = k // 2
        return lax.rem(z + jnp.where(lax.rem(k, 2) == 0, 8 + half, 8 - half), NZ)

    def z_id(zt):
        return (zt * NQ + q, t)

    def p_id(pt):
        return (z * NQ + pt // NT, lax.rem(pt, NT))

    def half_id(h, jt):
        return (z * NQ + (jt // NT) * 2 + h, lax.rem(jt, NT))

    barrier = pltpu.get_barrier_semaphore()

    def greet_z(k, c):
        pl.semaphore_signal(barrier, inc=1, device_id=z_id(z_peer(k)), device_id_type=MESH)
        return c

    def greet_p(k, c):
        pl.semaphore_signal(
            barrier, inc=1, device_id=p_id(lax.rem(p + k, NP)), device_id_type=MESH
        )
        return c

    lax.fori_loop(1, NZ, greet_z, 0)
    lax.fori_loop(1, NP, greet_p, 0)
    stat_copy.start()

    def remote(src, dst, ssem, rsem, device):
        return pltpu.make_async_remote_copy(
            src_ref=src, dst_ref=dst, send_sem=ssem, recv_sem=rsem,
            device_id=device, device_id_type=MESH,
        )

    def z_send(phase, src, dst):
        def step(k, c):
            zt = z_peer(k)
            remote(src.at[zt], dst.at[z], z_ssem.at[phase], z_rsem.at[phase], z_id(zt)).start()
            return c

        lax.fori_loop(1, NZ, step, 0)
        dst[pl.ds(z, 1)] = src[pl.ds(z, 1)]

    def z_wait(phase, dst):
        part = dst.at[pl.ds(0, NZ - 1)]
        remote(part, part, z_ssem.at[phase], z_rsem.at[phase], z_id(z)).wait_recv()

    def z_drain(phase, src):
        part = src.at[pl.ds(0, NZ - 1)]
        remote(part, part, z_ssem.at[phase], z_rsem.at[phase], z_id(z)).wait_send()

    def p_send(phase, src, dst):
        def step(k, c):
            pt = lax.rem(p + k, NP)
            remote(src.at[pt], dst.at[p], p_ssem.at[phase], p_rsem.at[phase], p_id(pt)).start()
            return c

        lax.fori_loop(1, NP, step, 0)
        dst[pl.ds(p, 1)] = src[pl.ds(p, 1)]

    def p_wait(phase, dst, count):
        part = dst.at[pl.ds(0, count)]
        remote(part, part, p_ssem.at[phase], p_rsem.at[phase], p_id(p)).wait_recv()

    def p_drain(phase, src, count):
        part = src.at[pl.ds(0, count)]
        remote(part, part, p_ssem.at[phase], p_rsem.at[phase], p_id(p)).wait_send()

    def to_half(phase, h, src, dst):
        def send(jt):
            remote(
                src.at[jt], dst.at[p], p_ssem.at[phase], p_rsem.at[phase], half_id(h, jt)
            ).start()

        def step(k, c):
            send(lax.rem(j + k, HALF))
            return c

        lax.fori_loop(1, HALF, step, 0)

        @pl.when(core != h)
        def _():
            send(j)

        @pl.when(core == h)
        def _():
            dst[pl.ds(p, 1)] = src[pl.ds(j, 1)]

    def to_half_drain(phase, h, src):
        @pl.when(core == h)
        def _():
            p_drain(phase, src, HALF - 1)

        @pl.when(core != h)
        def _():
            p_drain(phase, src, HALF)

    def from_half(phase, src, dst):
        def step(k, c):
            pt = lax.rem(p + k, NP)
            remote(src.at[pt], dst.at[j], p_ssem.at[phase], p_rsem.at[phase], p_id(pt)).start()
            return c

        lax.fori_loop(1, NP, step, 0)
        dst[pl.ds(j, 1)] = src[pl.ds(p, 1)]

    def from_half_wait(phase, h, dst):
        @pl.when(core == h)
        def _():
            p_wait(phase, dst, HALF - 1)

        @pl.when(core != h)
        def _():
            p_wait(phase, dst, HALF)

    i0 = iota((n, n), 0)
    i1 = iota((n, n), 1)
    owner_row_i = owner_ref[...]
    owner_row = owner_row_i.astype(F32)
    owner_col = jnp.sum(jnp.where(i0 == i1, owner_row, 0.0), axis=1, keepdims=True)
    owner_col_i = owner_col.astype(jnp.int32)
    same = owner_col == owner_row
    rank_row = jnp.sum(ones_where(same & (i0 < i1)), axis=0, keepdims=True)
    rank_col = jnp.sum(ones_where(same & (i1 < i0)), axis=1, keepdims=True)

    def first_key(owner):
        place = (lax.shift_right_logical(owner, 4) & 1) * NT + (owner & (NT - 1))
        chunk = 1 + (lax.shift_right_logical(owner, 3) & 1)
        return chunk * m + lax.shift_right_logical(owner, 5) * HALF + place

    plane_row = jnp.floor(owner_row * (1.0 / NP))
    plane_col = jnp.floor(owner_col * (1.0 / NP))
    pos_row = jnp.sum(
        ones_where(
            (jnp.where(rank_col > 0.5, plane_col, -2.0) == jnp.where(rank_row > 0.5, plane_row, -1.0))
            & (i0 < i1)
        ),
        axis=0,
        keepdims=True,
    )
    pos_col = jnp.sum(
        ones_where(
            (jnp.where(rank_col > 0.5, plane_col, -1.0) == jnp.where(rank_row > 0.5, plane_row, -2.0))
            & (i1 < i0)
        ),
        axis=1,
        keepdims=True,
    )

    def keys(owner_i, rank, plane, pos):
        second = jnp.where(pos < CAP1 - 0.5, plane * CAP1 + pos, -1.0)
        return jnp.where(rank > 0.5, second, first_key(owner_i).astype(F32))

    key_row = keys(owner_row_i, rank_row, plane_row, pos_row)
    key_col = keys(owner_col_i, rank_col, plane_col, pos_col)

    grad_copy.wait()
    h0 = iota((m, n), 0).astype(F32)
    for chunk in range(3):
        pick = ones_where(key_row == h0 + float(chunk * m)).astype(BF16)
        z_out[chunk] = dot(pick, grad_v[...]).astype(BF16).reshape(NZ, HALF, n)
        if chunk == 0:
            pl.semaphore_wait(barrier, NZ - 1 + NP - 1)
        z_send(chunk, z_out.at[chunk], z_in.at[chunk])

    final_ref[...] = ones_where(key_col == iota((n, 3 * m), 1).astype(F32)).astype(BF16)
    flag_ref[0, 0] = jnp.max(jnp.where(rank_row > 0.5, pos_row, 0.0))

    def fold_table(size, places):
        a, b = iota((size, size), 0), iota((size, size), 1)
        there = (a & (NZ - 1)) * places + lax.shift_right_logical(a, 4)
        back = (b & (NZ - 1)) * places + lax.shift_right_logical(b, 4)
        return ones_where(there == b).astype(BF16), ones_where(back == a).astype(BF16)

    fold_ref[...], unfold_ref[...] = fold_table(n, NP)
    fold_half[...], unfold_half[...] = fold_table(m, HALF)

    z_base = (z * NP).astype(F32)
    dev_of = z_base + lax.shift_right_logical(i0, 4).astype(F32)
    dev_of_t = z_base + lax.shift_right_logical(i1, 4).astype(F32)
    held_row = jnp.where(rank_row > 0.5, owner_row, -1.0)
    held_col = jnp.where(rank_col > 0.5, owner_col, -1.0)
    at_col = jnp.sum(jnp.where(held_row == dev_of, pos_row + 1.0, 0.0), axis=1, keepdims=True)
    at_row = jnp.sum(jnp.where(held_col == dev_of_t, pos_col + 1.0, 0.0), axis=0, keepdims=True)
    a0, a1 = iota((n, m), 0), iota((n, m), 1)
    place_ref[...] = ones_where(
        (lax.shift_right_logical(a1, 4) == (a0 & (NZ - 1)))
        & ((a1 & (CAP1 - 1)).astype(F32) == at_col - 1.0)
    ).astype(BF16)
    c0, c1 = iota((m, n), 0), iota((m, n), 1)
    place_t_ref[...] = ones_where(
        (lax.shift_right_logical(c0, 4) == (c1 & (NZ - 1)))
        & ((c0 & (CAP1 - 1)).astype(F32) == at_row - 1.0)
    ).astype(BF16)
    norm_mine[...] = jnp.zeros_like(norm_mine)

    me_f = me.astype(F32)
    lane = iota((1, n), 1)
    identity5 = jnp.where(i0 == i1, 1.25, 0.0)

    def all_sum(x):
        return jnp.sum(jnp.sum(x, axis=1, keepdims=True), axis=0, keepdims=True)

    def inverse_root(stat):
        norm_scale = jnp.sqrt(all_sum(stat * stat))
        matrix = stat * (1.0 / norm_scale)
        factor = identity5 - 0.25 * matrix
        low = factor.astype(BF16)
        root = (lax.rsqrt(jnp.sqrt(norm_scale)) * factor).astype(BF16)
        square = dot(low, low).astype(BF16)
        fourth = dot(square, square).astype(BF16)
        matrix = dot(fourth, matrix.astype(BF16))
        factor = (identity5 - 0.25 * matrix).astype(BF16)
        return dot(root, factor).astype(BF16)

    def owner_work(slot, incoming, outgoing):
        block = dot(unfold_ref[...], incoming[...].reshape(n, n)).astype(BF16)
        block_ref[...] = block
        eye = ones_where(i0 == i1).astype(BF16)
        block_t = dot_t(eye, block).astype(BF16)
        right = inverse_root(DECAY * stats_v[slot, 1].astype(F32) + dot_t(block_t, block_t))
        middle = dot(block_ref[...], right).astype(BF16)
        left = inverse_root(
            DECAY * stats_v[slot, 0].astype(F32) + dot_t(block_ref[...], block_ref[...])
        )
        raw = dot(left, middle)
        here = (owner_row == me_f) & (jnp.abs(rank_row - float(slot)) < 0.5)
        used = all_sum(ones_where(here))
        layer1 = all_sum(ones_where(here & (lane >= n // 2)))
        raw_ref[...] = jnp.where(used > 0.5, raw, 0.0).astype(BF16)
        outgoing[...] = dot(fold_ref[...], raw_ref[...]).astype(BF16).reshape(NP, NZ, n)

        def tally():
            raw_f = raw_ref[...].astype(F32)
            block_f = block_ref[...].astype(F32)
            layer = jnp.where(layer1 > 0.5, 1, 0)
            s0 = iota((8, 128), 0)
            sums = jnp.where(s0 == layer, all_sum(block_f * block_f), 0.0)
            sums = sums + jnp.where(s0 == layer + 2, all_sum(raw_f * raw_f), 0.0)
            norm_mine[...] = norm_mine[...] + sums

        return tally

    z_wait(0, z_in.at[0])
    pb_out[...] = dot(place_ref[...], z_in[0].reshape(m, n)).astype(BF16).reshape(NP, NZ, n)
    p_send(0, pb_out, pb_in)

    def fold_in(h):
        z_wait(1 + h, z_in.at[1 + h])
        rows = dot(fold_half[...], z_in[1 + h].reshape(m, n)).astype(BF16)
        pa_out[h] = rows.reshape(HALF, NZ, n)
        to_half(1 + h, h, pa_out.at[h], pa_in)

    def fold_out(h):
        from_half_wait(4 + h, h, ra_in.at[h])
        rows = dot(unfold_half[...], ra_in[h].reshape(m, n)).astype(BF16)
        y_out[1 + h] = rows.reshape(NZ, HALF, n)
        z_send(4 + h, y_out.at[1 + h], y_in.at[1 + h])

    def first_work(h):
        @pl.when(core == h)
        def _():
            p_wait(1 + h, pa_in, NP - 1)
            tally = owner_work(0, pa_in, ra_out)
            from_half(4 + h, ra_out, ra_in.at[h])
            tally()

    fold_in(0)
    stat_copy.wait()
    p_wait(0, pb_in, NP - 1)
    tally = owner_work(1, pb_in, rb_out)
    p_send(3, rb_out, rb_in)
    tally()
    fold_in(1)
    first_work(0)

    p_wait(3, rb_in, NP - 1)
    rows = dot(place_t_ref[...], rb_in[...].reshape(n, n)).astype(BF16)
    y_out[0] = rows.reshape(NZ, HALF, n)
    z_send(3, y_out.at[0], y_in.at[0])

    first_work(1)

    def norm_step(k, c):
        pt = lax.rem(p + k, NP)
        remote(norm_mine, norm_plane.at[p], p_ssem.at[6], p_rsem.at[6], p_id(pt)).start()
        return c

    lax.fori_loop(1, NP, norm_step, 0)
    norm_plane[pl.ds(p, 1)] = norm_mine[...][None]

    fold_out(0)

    p_wait(6, norm_plane, NP - 1)
    plane_mine[...] = jnp.sum(norm_plane[...], axis=0)

    def plane_step(k, c):
        zt = z_peer(k)
        remote(plane_mine, plane_all.at[z], z_ssem.at[6], z_rsem.at[6], z_id(zt)).start()
        return c

    lax.fori_loop(1, NZ, plane_step, 0)
    plane_all[pl.ds(z, 1)] = plane_mine[...][None]

    fold_out(1)

    def returned(chunk):
        z_wait(3 + chunk, y_in.at[chunk])
        return dot(final_ref[:, chunk * m : (chunk + 1) * m], y_in[chunk].reshape(m, n))

    rows_ref[...] = returned(0)
    rows_ref[...] = rows_ref[...] + returned(1)
    z_wait(6, plane_all)
    totals = jnp.sum(plane_all[...], axis=0)
    ratio0 = jnp.sqrt(totals[0:1, 0:1] / (totals[2:3, 0:1] + GRAFT_EPS))
    ratio1 = jnp.sqrt(totals[1:2, 0:1] / (totals[3:4, 0:1] + GRAFT_EPS))
    ratio = jnp.where(iota((n, 1), 0) < n // 2, ratio0, ratio1)
    out_ref[...] = ((rows_ref[...] + returned(2)) * ratio).astype(BF16)

    for chunk in range(3):
        z_drain(chunk, z_out.at[chunk])
        z_drain(3 + chunk, y_out.at[chunk])
    z_drain(6, plane_all)
    p_drain(0, pb_out, NP - 1)
    p_drain(3, rb_out, NP - 1)
    p_drain(6, norm_plane, NP - 1)
    for h in range(2):
        to_half_drain(1 + h, h, pa_out.at[h])

        @pl.when(core == h)
        def _():
            p_drain(4 + h, ra_out, NP - 1)


def fast_program(gradient, owner_table, prev_stats):
    n = BLK
    m = NZ * HALF
    chunks = pltpu.VMEM((3, NZ, HALF, n), BF16)
    plane = pltpu.VMEM((NP, NZ, n), BF16)
    halves = pltpu.VMEM((2, HALF, NZ, n), BF16)
    square = pltpu.VMEM((n, n), BF16)
    vmem = pl.BlockSpec(memory_space=pltpu.VMEM)
    hbm = pl.BlockSpec(memory_space=pl.ANY)
    return pl.pallas_call(
        kernel,
        out_shape=(
            jax.ShapeDtypeStruct((n, n), BF16),
            jax.ShapeDtypeStruct((1, 1), F32),
        ),
        in_specs=[hbm, vmem, hbm],
        out_specs=(vmem, pl.BlockSpec(memory_space=pltpu.SMEM)),
        scratch_shapes=[
            square,
            pltpu.VMEM((2, 2, n, n), BF16),
            chunks, chunks,
            plane, plane, halves, plane,
            plane, plane, plane, halves,
            chunks, chunks,
            pltpu.VMEM((8, 128), F32),
            pltpu.VMEM((NP, 8, 128), F32),
            pltpu.VMEM((8, 128), F32),
            pltpu.VMEM((NZ, 8, 128), F32),
            square, square,
            pltpu.VMEM((m, m), BF16),
            pltpu.VMEM((m, m), BF16),
            pltpu.VMEM((n, m), BF16),
            pltpu.VMEM((m, n), BF16),
            pltpu.VMEM((n, 3 * m), BF16),
            square, square,
            pltpu.VMEM((n, n), F32),
            pltpu.SemaphoreType.DMA((2,)),
            pltpu.SemaphoreType.DMA((7,)),
            pltpu.SemaphoreType.DMA((7,)),
            pltpu.SemaphoreType.DMA((7,)),
            pltpu.SemaphoreType.DMA((7,)),
        ],
        compiler_params=pltpu.CompilerParams(
            collective_id=0, has_side_effects=True, vmem_limit_bytes=62 << 20
        ),
    )(gradient, owner_table.reshape(1, -1), prev_stats)


def on_device(gradient, owner_table, prev_stats):
    update, overflow = fast_program(gradient, owner_table, prev_stats)
    return lax.cond(
        overflow[0, 0] > CAP1 - 0.5,
        lambda g, o, s, u: general_program(g, o, s),
        lambda g, o, s, u: u,
        gradient,
        owner_table,
        prev_stats,
        update,
    )


def solution(mesh):
    in_specs = (P(None, ("dp", "tensor")), P(), P(("dp", "tensor"), None, None, None))
    out_specs = P(None, ("dp", "tensor"))
    return jax.shard_map(
        on_device, mesh=mesh, in_specs=in_specs, out_specs=out_specs, check_vma=False
    )
```

time: 119 us -> 101 us (0.85)
  Pallas kernels: 115 us -> 98.8 us
  local copies, waits for them, and re-layouts: 2 us -> 0.8 us
    pallas_call x1, Pallas kernels: 115 us -> 98.8 us  [fast_program(): pl.pallas_call(kernel, out_shape=(jax.ShapeDtypeStruct((n, n), BF16), jax...]
    slice x1 -> x0, local copies, waits for them, and re-layouts: 1.19 us -> none  [on_device(): overflow[0, 0] > CAP1 - 0.5]
where the time goes in v2:
time: 101 us
  Pallas kernels  98.8 us (98%)
    pallas_call x1, Pallas kernels, fast_program(): pl.pallas_call(kernel, out_shape=(jax.ShapeDtypeStruct((n, n), BF16), jax...  98.8 us

profile of v2, /device:TPU:1, one launch (start us, length us, event | category | flops | bytes accessed | tf_op | source)
XLA Modules:
  0.0 100.6 jit_solution(13038337018047731445)
XLA Ops:
  0.0 0.0 copy-start.8
  0.0 0.0 copy-start
  0.0 98.8 %shard_map.39 = (bf16[512,512]{1,0:T(8,128)(2,1)S(1)}, f32[1,1]{1,0:T(1,128)}) custom-call(bf16[512,512]{1,0:T(8,128)(2,1)} %grad_hbm.1, s32[1,512]{1,0:T(1,128)} %bitcast.30, bf16[2,2,512,512]{3,2,1,0:T(8,128)(2,1)} %stats_hbm.1), custom_call_target="tpu_custom_call" | custom-call | tf_op jit(solution)/shard_map/pallas_call | solution.py:493
  99.5 0.0 copy-done.8
  99.5 0.0 copy-done
  99.6 0.3 conditional.1
  99.8 0.8 copy.88
Async XLA Ops:
  0.0 99.5 %copy-start.8 = (s32[512]{0:T(512)S(1)}, s32[512]{0:T(512)}, u32[]{:S(2)}) copy-start(s32[512]{0:T(512)} %param.6) | copy-start | bytes 6148
  0.0 99.5 %copy-start = (bf16[512,512]{1,0:T(8,128)(2,1)S(1)}, bf16[512,512]{1,0:T(8,128)(2,1)}, u32[]{:S(2)}) copy-start(bf16[512,512]{1,0:T(8,128)(2,1)} %grad_hbm.1) | copy-start | bytes 1572868

commit v3 on v2

--- a/solution.py
+++ b/solution.py
@@ -274,7 +274,7 @@
 
     def first_key(owner):
         place = (lax.shift_right_logical(owner, 4) & 1) * NT + (owner & (NT - 1))
-        chunk = 1 + (lax.shift_right_logical(owner, 3) & 1)
+        chunk = lax.shift_right_logical(owner, 3) & 1
         return chunk * m + lax.shift_right_logical(owner, 5) * HALF + place
 
     plane_row = jnp.floor(owner_row * (1.0 / NP))
@@ -297,7 +297,7 @@
     )
 
     def keys(owner_i, rank, plane, pos):
-        second = jnp.where(pos < CAP1 - 0.5, plane * CAP1 + pos, -1.0)
+        second = jnp.where(pos < CAP1 - 0.5, plane * CAP1 + pos + float(2 * m), -1.0)
         return jnp.where(rank > 0.5, second, first_key(owner_i).astype(F32))
 
     key_row = keys(owner_row_i, rank_row, plane_row, pos_row)
@@ -350,28 +350,32 @@
     def all_sum(x):
         return jnp.sum(jnp.sum(x, axis=1, keepdims=True), axis=0, keepdims=True)
 
-    def inverse_root(stat):
-        norm_scale = jnp.sqrt(all_sum(stat * stat))
-        matrix = stat * (1.0 / norm_scale)
-        factor = identity5 - 0.25 * matrix
-        low = factor.astype(BF16)
-        root = (lax.rsqrt(jnp.sqrt(norm_scale)) * factor).astype(BF16)
-        square = dot(low, low).astype(BF16)
-        fourth = dot(square, square).astype(BF16)
-        matrix = dot(fourth, matrix.astype(BF16))
-        factor = (identity5 - 0.25 * matrix).astype(BF16)
-        return dot(root, factor).astype(BF16)
+    def inverse_roots_of(stats):
+        scales = [jnp.sqrt(all_sum(stat * stat)) for stat in stats]
+        matrices = [stat * (1.0 / scale) for stat, scale in zip(stats, scales)]
+        factors = [identity5 - 0.25 * matrix for matrix in matrices]
+        lows = [factor.astype(BF16) for factor in factors]
+        squares = [dot(low, low).astype(BF16) for low in lows]
+        roots = [
+            (lax.rsqrt(jnp.sqrt(scale)) * factor).astype(BF16)
+            for scale, factor in zip(scales, factors)
+        ]
+        fourths = [dot(square, square).astype(BF16) for square in squares]
+        matrices = [
+            dot(fourth, matrix.astype(BF16)) for fourth, matrix in zip(fourths, matrices)
+        ]
+        factors = [(identity5 - 0.25 * matrix).astype(BF16) for matrix in matrices]
+        return [dot(root, factor).astype(BF16) for root, factor in zip(roots, factors)]
 
     def owner_work(slot, incoming, outgoing):
-        block = dot(unfold_ref[...], incoming[...].reshape(n, n)).astype(BF16)
-        block_ref[...] = block
+        folded = incoming[...].reshape(n, n)
         eye = ones_where(i0 == i1).astype(BF16)
-        block_t = dot_t(eye, block).astype(BF16)
-        right = inverse_root(DECAY * stats_v[slot, 1].astype(F32) + dot_t(block_t, block_t))
+        block_t = dot_t(eye, folded).astype(BF16)
+        block_ref[...] = dot(unfold_ref[...], folded).astype(BF16)
+        right_stat = DECAY * stats_v[slot, 1].astype(F32) + dot_t(block_t, block_t)
+        left_stat = DECAY * stats_v[slot, 0].astype(F32) + dot_t(block_ref[...], block_ref[...])
+        right, left = inverse_roots_of([right_stat, left_stat])
         middle = dot(block_ref[...], right).astype(BF16)
-        left = inverse_root(
-            DECAY * stats_v[slot, 0].astype(F32) + dot_t(block_ref[...], block_ref[...])
-        )
         raw = dot(left, middle)
         here = (owner_row == me_f) & (jnp.abs(rank_row - float(slot)) < 0.5)
         used = all_sum(ones_where(here))
@@ -390,21 +394,17 @@
 
         return tally
 
-    z_wait(0, z_in.at[0])
-    pb_out[...] = dot(place_ref[...], z_in[0].reshape(m, n)).astype(BF16).reshape(NP, NZ, n)
-    p_send(0, pb_out, pb_in)
-
     def fold_in(h):
-        z_wait(1 + h, z_in.at[1 + h])
-        rows = dot(fold_half[...], z_in[1 + h].reshape(m, n)).astype(BF16)
+        z_wait(h, z_in.at[h])
+        rows = dot(fold_half[...], z_in[h].reshape(m, n)).astype(BF16)
         pa_out[h] = rows.reshape(HALF, NZ, n)
         to_half(1 + h, h, pa_out.at[h], pa_in)
 
     def fold_out(h):
         from_half_wait(4 + h, h, ra_in.at[h])
         rows = dot(unfold_half[...], ra_in[h].reshape(m, n)).astype(BF16)
-        y_out[1 + h] = rows.reshape(NZ, HALF, n)
-        z_send(4 + h, y_out.at[1 + h], y_in.at[1 + h])
+        y_out[h] = rows.reshape(NZ, HALF, n)
+        z_send(3 + h, y_out.at[h], y_in.at[h])
 
     def first_work(h):
         @pl.when(core == h)
@@ -416,19 +416,21 @@
 
     fold_in(0)
     stat_copy.wait()
+    first_work(0)
+    fold_in(1)
+    first_work(1)
+
+    z_wait(2, z_in.at[2])
+    pb_out[...] = dot(place_ref[...], z_in[2].reshape(m, n)).astype(BF16).reshape(NP, NZ, n)
+    p_send(0, pb_out, pb_in)
+
+    fold_out(0)
+    fold_out(1)
+
     p_wait(0, pb_in, NP - 1)
     tally = owner_work(1, pb_in, rb_out)
     p_send(3, rb_out, rb_in)
     tally()
-    fold_in(1)
-    first_work(0)
-
-    p_wait(3, rb_in, NP - 1)
-    rows = dot(place_t_ref[...], rb_in[...].reshape(n, n)).astype(BF16)
-    y_out[0] = rows.reshape(NZ, HALF, n)
-    z_send(3, y_out.at[0], y_in.at[0])
-
-    first_work(1)
 
     def norm_step(k, c):
         pt = lax.rem(p + k, NP)
@@ -438,7 +440,10 @@
     lax.fori_loop(1, NP, norm_step, 0)
     norm_plane[pl.ds(p, 1)] = norm_mine[...][None]
 
-    fold_out(0)
+    p_wait(3, rb_in, NP - 1)
+    rows = dot(place_t_ref[...], rb_in[...].reshape(n, n)).astype(BF16)
+    y_out[2] = rows.reshape(NZ, HALF, n)
+    z_send(5, y_out.at[2], y_in.at[2])
 
     p_wait(6, norm_plane, NP - 1)
     plane_mine[...] = jnp.sum(norm_plane[...], axis=0)
@@ -450,8 +455,6 @@
 
     lax.fori_loop(1, NZ, plane_step, 0)
     plane_all[pl.ds(z, 1)] = plane_mine[...][None]
-
-    fold_out(1)
 
     def returned(chunk):
         z_wait(3 + chunk, y_in.at[chunk])
@@ -524,7 +527,7 @@
             pltpu.SemaphoreType.DMA((7,)),
         ],
         compiler_params=pltpu.CompilerParams(
-            collective_id=0, has_side_effects=True, vmem_limit_bytes=62 << 20
+            collective_id=0, has_side_effects=True, vmem_limit_bytes=63 << 20
         ),
     )(gradient, owner_table.reshape(1, -1), prev_stats)
 

time: 101 us -> 103 us (1.020)
  local copies, waits for them, and re-layouts: 0.8 us -> 1.88 us
    unnamed x5, local copies, waits for them, and re-layouts: 0.8 us -> 1.88 us
where the time goes in v3:
time: 103 us
  Pallas kernels  99.7 us (97%)
  local copies, waits for them, and re-layouts  1.88 us (2%)
    pallas_call x1, Pallas kernels, fast_program(): pl.pallas_call(kernel, out_shape=(jax.ShapeDtypeStruct((n, n), BF16), jax...  99.7 us

profile of v3, /device:TPU:1, one launch (start us, length us, event | category | flops | bytes accessed | tf_op | source)
XLA Modules:
  0.0 102.6 jit_solution(3731588424824773918)
XLA Ops:
  0.0 0.0 copy-start.8
  0.0 0.0 copy-start
  0.0 99.7 %shard_map.39 = (bf16[512,512]{1,0:T(8,128)(2,1)}, f32[1,1]{1,0:T(1,128)}) custom-call(bf16[512,512]{1,0:T(8,128)(2,1)} %grad_hbm.1, s32[1,512]{1,0:T(1,128)} %bitcast.30, bf16[2,2,512,512]{3,2,1,0:T(8,128)(2,1)} %stats_hbm.1), custom_call_target="tpu_custom_call" | custom-call | tf_op jit(solution)/shard_map/pallas_call | solution.py:496
  100.4 0.0 copy-done.8
  100.5 0.0 copy-done
  100.5 0.3 conditional.1
  100.7 1.9 %copy.88 = bf16[512,512]{1,0:T(8,128)(2,1)} copy(bf16[512,512]{1,0:T(8,128)(2,1)} %get-tuple-element.22) | data formatting | bytes 1048576
Async XLA Ops:
  0.0 100.4 %copy-start.8 = (s32[512]{0:T(512)S(1)}, s32[512]{0:T(512)}, u32[]{:S(2)}) copy-start(s32[512]{0:T(512)} %param.6) | copy-start | bytes 6148
  0.0 100.5 %copy-start = (bf16[512,512]{1,0:T(8,128)(2,1)S(1)}, bf16[512,512]{1,0:T(8,128)(2,1)}, u32[]{:S(2)}) copy-start(bf16[512,512]{1,0:T(8,128)(2,1)} %grad_hbm.1) | copy-start | bytes 1572868

commit v4 on v3

--- a/solution.py
+++ b/solution.py
@@ -274,7 +274,7 @@
 
     def first_key(owner):
         place = (lax.shift_right_logical(owner, 4) & 1) * NT + (owner & (NT - 1))
-        chunk = lax.shift_right_logical(owner, 3) & 1
+        chunk = 1 + (lax.shift_right_logical(owner, 3) & 1)
         return chunk * m + lax.shift_right_logical(owner, 5) * HALF + place
 
     plane_row = jnp.floor(owner_row * (1.0 / NP))
@@ -297,7 +297,7 @@
     )
 
     def keys(owner_i, rank, plane, pos):
-        second = jnp.where(pos < CAP1 - 0.5, plane * CAP1 + pos + float(2 * m), -1.0)
+        second = jnp.where(pos < CAP1 - 0.5, plane * CAP1 + pos, -1.0)
         return jnp.where(rank > 0.5, second, first_key(owner_i).astype(F32))
 
     key_row = keys(owner_row_i, rank_row, plane_row, pos_row)
@@ -394,17 +394,21 @@
 
         return tally
 
+    z_wait(0, z_in.at[0])
+    pb_out[...] = dot(place_ref[...], z_in[0].reshape(m, n)).astype(BF16).reshape(NP, NZ, n)
+    p_send(0, pb_out, pb_in)
+
     def fold_in(h):
-        z_wait(h, z_in.at[h])
-        rows = dot(fold_half[...], z_in[h].reshape(m, n)).astype(BF16)
+        z_wait(1 + h, z_in.at[1 + h])
+        rows = dot(fold_half[...], z_in[1 + h].reshape(m, n)).astype(BF16)
         pa_out[h] = rows.reshape(HALF, NZ, n)
         to_half(1 + h, h, pa_out.at[h], pa_in)
 
     def fold_out(h):
         from_half_wait(4 + h, h, ra_in.at[h])
         rows = dot(unfold_half[...], ra_in[h].reshape(m, n)).astype(BF16)
-        y_out[h] = rows.reshape(NZ, HALF, n)
-        z_send(3 + h, y_out.at[h], y_in.at[h])
+        y_out[1 + h] = rows.reshape(NZ, HALF, n)
+        z_send(4 + h, y_out.at[1 + h], y_in.at[1 + h])
 
     def first_work(h):
         @pl.when(core == h)
@@ -416,21 +420,19 @@
 
     fold_in(0)
     stat_copy.wait()
-    first_work(0)
-    fold_in(1)
-    first_work(1)
-
-    z_wait(2, z_in.at[2])
-    pb_out[...] = dot(place_ref[...], z_in[2].reshape(m, n)).astype(BF16).reshape(NP, NZ, n)
-    p_send(0, pb_out, pb_in)
-
-    fold_out(0)
-    fold_out(1)
-
     p_wait(0, pb_in, NP - 1)
     tally = owner_work(1, pb_in, rb_out)
     p_send(3, rb_out, rb_in)
     tally()
+    first_work(0)
+    fold_in(1)
+
+    p_wait(3, rb_in, NP - 1)
+    rows = dot(place_t_ref[...], rb_in[...].reshape(n, n)).astype(BF16)
+    y_out[0] = rows.reshape(NZ, HALF, n)
+    z_send(3, y_out.at[0], y_in.at[0])
+
+    first_work(1)
 
     def norm_step(k, c):
         pt = lax.rem(p + k, NP)
@@ -440,10 +442,7 @@
     lax.fori_loop(1, NP, norm_step, 0)
     norm_plane[pl.ds(p, 1)] = norm_mine[...][None]
 
-    p_wait(3, rb_in, NP - 1)
-    rows = dot(place_t_ref[...], rb_in[...].reshape(n, n)).astype(BF16)
-    y_out[2] = rows.reshape(NZ, HALF, n)
-    z_send(5, y_out.at[2], y_in.at[2])
+    fold_out(0)
 
     p_wait(6, norm_plane, NP - 1)
     plane_mine[...] = jnp.sum(norm_plane[...], axis=0)
@@ -455,6 +454,8 @@
 
     lax.fori_loop(1, NZ, plane_step, 0)
     plane_all[pl.ds(z, 1)] = plane_mine[...][None]
+
+    fold_out(1)
 
     def returned(chunk):
         z_wait(3 + chunk, y_in.at[chunk])
@@ -527,7 +528,7 @@
             pltpu.SemaphoreType.DMA((7,)),
         ],
         compiler_params=pltpu.CompilerParams(
-            collective_id=0, has_side_effects=True, vmem_limit_bytes=63 << 20
+            collective_id=0, has_side_effects=True, vmem_limit_bytes=62 << 20
         ),
     )(gradient, owner_table.reshape(1, -1), prev_stats)
 

time: 103 us -> 101 us (0.981)
  local copies, waits for them, and re-layouts: 1.88 us -> 0.8 us
    unnamed x5, local copies, waits for them, and re-layouts: 1.88 us -> 0.8 us
    pallas_call x1, Pallas kernels: 99.7 us -> 98.7 us  [fast_program(): pl.pallas_call(kernel, out_shape=(jax.ShapeDtypeStruct((n, n), BF16), jax...]
where the time goes in v4:
time: 101 us; the launch traced here: 100 us
  Pallas kernels  98.7 us (98%)
    pallas_call x1, Pallas kernels, fast_program(): pl.pallas_call(kernel, out_shape=(jax.ShapeDtypeStruct((n, n), BF16), jax...  98.7 us

profile of v4, /device:TPU:1, one launch (start us, length us, event | category | flops | bytes accessed | tf_op | source)
XLA Modules:
  0.0 100.5 jit_solution(16439536836316159199)
XLA Ops:
  0.0 0.0 copy-start.8
  0.0 0.0 copy-start
  0.0 98.7 %shard_map.39 = (bf16[512,512]{1,0:T(8,128)(2,1)S(1)}, f32[1,1]{1,0:T(1,128)}) custom-call(bf16[512,512]{1,0:T(8,128)(2,1)} %grad_hbm.1, s32[1,512]{1,0:T(1,128)} %bitcast.30, bf16[2,2,512,512]{3,2,1,0:T(8,128)(2,1)} %stats_hbm.1), custom_call_target="tpu_custom_call" | custom-call | tf_op jit(solution)/shard_map/pallas_call | solution.py:497
  99.4 0.0 copy-done.8
  99.4 0.0 copy-done
  99.4 0.3 conditional.1
  99.7 0.8 copy.88
Async XLA Ops:
  0.0 99.4 %copy-start.8 = (s32[512]{0:T(512)S(1)}, s32[512]{0:T(512)}, u32[]{:S(2)}) copy-start(s32[512]{0:T(512)} %param.6) | copy-start | bytes 6148
  0.0 99.4 %copy-start = (bf16[512,512]{1,0:T(8,128)(2,1)S(1)}, bf16[512,512]{1,0:T(8,128)(2,1)}, u32[]{:S(2)}) copy-start(bf16[512,512]{1,0:T(8,128)(2,1)} %grad_hbm.1) | copy-start | bytes 1572868
